TPU v7x, 32 devices: a whole 2x2x4 slice. The times are simulated.
32 devices in a mesh: layer: 4 (over y, core), tx: 2 (over x), ty: 4 (over z).
Axes of the slice: x: 2, y: 2, z: 4, core: 2. Of those that a mesh axis runs over, the one named last changes fastest.
Arguments:
- layers: float32 [4, 256, 2048], P('layer', 'tx', 'ty'), may hold values from -6 to 6
- wind: int32 [4, 2], P('layer'), may hold values from -128 to 128
- offsets: int32 [4, 9, 2], P('layer'), may hold values from -64 to 64
- weights: bfloat16 [9, 2, 256, 2048], P(None, None, 'tx', 'ty'), may hold values from -0.5 to 0.5
- sub_index: int32 [256, 2048], P('tx', 'ty'), may hold values from -1 to 255, as said below
Outputs:
- slopes: float32 [2, 9, 32, 256], P(None, None, 'tx', 'ty')
Inputs may be any that keep to these rules, and one draw needn't show every extreme that they name: sub_index[i, j] is -1 or j // 8.
All inputs are finite; a program needn't handle non-finite values.
Results may differ from a plain program's by a relative error of at most 0.0003.
Values sent between devices are 32-bit elements; how exact they have to be, the bound alone decides.
A program may use at most 256 MiB of HBM per device.

v0:
```python
import functools

import jax
import jax.numpy as jnp
from jax import lax
from jax.experimental import pallas as pl
from jax.experimental.pallas import tpu as pltpu
from jax.sharding import PartitionSpec as P

DIRS = 9
SUB = 8
HMAX = 2
FOOT = 64
LANES = 128
RIM = 72
MESH = pl.DeviceIdType.MESH


def kernel(
    sizes, wind, offsets, layers, weights, sub_index, out, field, shifted, wraw, wlive, sub, parts,
    local_sem, xs_sem, xr_sem, zs_sem, zr_sem, ss_sem, sr_sem,
):
    n_layer, n_tx, n_ty = sizes
    rows, cols = sub_index.shape
    tiles = cols // LANES
    groups = rows // SUB
    last = tiles + 1
    foot_rows = RIM if n_tx > 2 else rows - RIM
    layer = lax.axis_index("layer")
    tx = lax.axis_index("tx")
    ty = lax.axis_index("ty")
    up = {"tx": lax.rem(tx + n_tx - 1, n_tx)}
    down = {"tx": lax.rem(tx + 1, n_tx)}
    left = {"ty": lax.rem(ty + n_ty - 1, n_ty)}
    right = {"ty": lax.rem(ty + 1, n_ty)}
    peers = [{"layer": lax.rem(layer + k, n_layer)} for k in range(1, n_layer)]

    order = [0, tiles - 1] + list(range(1, tiles - 1))
    own = {}
    for c in order:
        copy = pltpu.make_async_copy(
            layers.at[0, :, pl.ds(c * LANES, LANES)],
            field.at[c + 1, pl.ds(RIM, rows), :],
            local_sem.at[c],
        )
        copy.start()
        own[c] = copy
    sub_copy = pltpu.make_async_copy(sub_index, sub, local_sem.at[tiles])
    sub_copy.start()
    weight_copy = pltpu.make_async_copy(weights, wraw, local_sem.at[tiles + 1])
    weight_copy.start()

    barrier = pltpu.get_barrier_semaphore()
    greeted = [up, left, right] if n_tx == 2 else [up, down, left, right]
    for device in greeted + peers:
        pl.semaphore_signal(barrier, inc=1, device_id=device, device_id_type=MESH)
    pl.semaphore_wait(barrier, len(greeted) + len(peers))

    def send(src, dst, send_sem, recv_sem, device):
        copy = pltpu.make_async_remote_copy(
            src_ref=src, dst_ref=dst, send_sem=send_sem, recv_sem=recv_sem,
            device_id=device, device_id_type=MESH,
        )
        copy.start()
        return copy

    def send_rows(c):
        return [
            send(
                field.at[c, pl.ds(rows, RIM), :], field.at[c, pl.ds(0, RIM), :],
                xs_sem.at[c - 1, 0], xr_sem.at[c - 1, 0], down,
            ),
            send(
                field.at[c, pl.ds(RIM, foot_rows), :], field.at[c, pl.ds(RIM + rows, foot_rows), :],
                xs_sem.at[c - 1, 1], xr_sem.at[c - 1, 1], up,
            ),
        ]

    def send_cols(start, size, k):
        return [
            send(
                field.at[tiles, pl.ds(start, size), :], field.at[0, pl.ds(start, size), :],
                zs_sem.at[0, k], zr_sem.at[0, k], right,
            ),
            send(
                field.at[1, pl.ds(start, size), :], field.at[last, pl.ds(start, size), :],
                zs_sem.at[1, k], zr_sem.at[1, k], left,
            ),
        ]

    edge_copies, mid_copies = [], []
    for c in order[:2]:
        own[c].wait()
        edge_copies += send_rows(c + 1)
    col_copies = send_cols(RIM, rows, 0)
    for c in order[2:]:
        own[c].wait()
        mid_copies += send_rows(c + 1)

    sub_copy.wait()
    weight_copy.wait()

    def prepare(d, carry):
        for c in range(tiles):
            for g in range(0, groups, 2):
                live = (sub[pl.ds(g * SUB, 2 * SUB), pl.ds(c * LANES, LANES)] >= 0).astype(jnp.float32)
                for s in range(2):
                    both = wraw[d, s, pl.ds(g * SUB, 2 * SUB), pl.ds(c * LANES, LANES)].astype(jnp.float32) * live
                    for h in range(2):
                        wlive[d, s, c, pl.ds(g + h, SUB, stride=groups), :] = both[h * SUB : (h + 1) * SUB]
        return carry

    lax.fori_loop(0, 4, prepare, 0)
    for copy in edge_copies:
        copy.wait_recv()
    col_copies += send_cols(0, RIM, 1) + send_cols(RIM + rows, foot_rows, 2)
    lax.fori_loop(4, DIRS, prepare, 0)

    for copy in mid_copies:
        copy.wait_recv()
    for copy in col_copies:
        copy.wait_recv()
    if n_tx == 2:
        for c in range(tiles + 2):
            field[c, pl.ds(RIM + rows + foot_rows, RIM - foot_rows), :] = field[c, pl.ds(0, RIM - foot_rows), :]

    wide = rows // SUB + 2 * FOOT // SUB
    qrow = lax.shift_right_arithmetic(wind[0, 0], 6)
    qcol = lax.shift_right_arithmetic(wind[0, 1], 6)
    frow = (wind[0, 0] - 64 * qrow).astype(jnp.float32) / 64.0
    fcol = (wind[0, 1] - 64 * qcol).astype(jnp.float32) / 64.0
    lead = HMAX + 1 - qcol
    lane = lax.broadcasted_iota(jnp.int32, (wide, LANES), 1)

    def shift_phase(p, carry):
        mixed = []
        for c in range(tiles + 2):
            here = field[c, pl.ds(RIM - FOOT + p - qrow, wide, stride=SUB), :]
            above = field[c, pl.ds(RIM - FOOT - 1 + p - qrow, wide, stride=SUB), :]
            mixed.append((1.0 - frow) * here + frow * above)
        first = [pltpu.roll(m, (LANES - lead) & (LANES - 1), 1) for m in mixed]
        second = [pltpu.roll(m, (LANES + 1 - lead) & (LANES - 1), 1) for m in mixed]
        for c in range(tiles + 2):
            after = min(c + 1, last)
            one = jnp.where(lane < LANES - lead, first[c], first[after])
            two = jnp.where(lane < LANES + 1 - lead, second[c], second[after])
            shifted[c, p, :, :] = (1.0 - fcol) * one + fcol * two
        return carry

    lax.fori_loop(0, SUB, shift_phase, 0)

    lane_g = lax.broadcasted_iota(jnp.int32, (groups, LANES), 1)
    half = cols // SUB
    pick_row = lax.broadcasted_iota(jnp.int32, (cols, LANES), 0)
    pick_col = lax.broadcasted_iota(jnp.int32, (cols, LANES), 1)
    pick = (lax.shift_right_logical(pick_row, 3) == (pick_col & (half - 1))).astype(jnp.bfloat16)

    def slopes(d, carry):
        top = offsets[0, 0, d] + FOOT
        begin = offsets[0, 1, d] + LANES - HMAX - 1
        base = lax.shift_right_arithmetic(begin, 7)
        skip = begin & (LANES - 1)
        turn = (LANES - skip) & (LANES - 1)
        sums = [[None] * tiles for _ in range(2)]
        for r in range(SUB):
            row = top + r
            phase = row & (SUB - 1)
            first = lax.shift_right_arithmetic(row, 3)
            turned = [
                pltpu.roll(shifted[base + c, phase, pl.ds(first, groups), :], turn, 1) for c in range(tiles + 1)
            ]
            for c in range(tiles):
                view = jnp.where(lane_g < LANES - skip, turned[c], turned[c + 1])
                for s in range(2):
                    term = wlive[d, s, c, pl.ds(r * groups, groups), :] * view
                    sums[s][c] = term if r == 0 else sums[s][c] + term
        rows_of = []
        for s in range(2):
            total = jnp.concatenate(sums[s], axis=1)
            high = total.astype(jnp.bfloat16)
            low = (total - high.astype(jnp.float32)).astype(jnp.bfloat16)
            rows_of += [high, low]
        added = jnp.dot(jnp.concatenate(rows_of, axis=0), pick, preferred_element_type=jnp.float32)
        one = added[0:groups] + added[groups : 2 * groups]
        two = added[2 * groups : 3 * groups] + added[3 * groups : 4 * groups]
        parts[layer, d, :, :] = jnp.where(lane_g < half, one, two)
        return carry

    sum_copies = []
    cuts = [0, 4, 7, DIRS]
    for b in range(3):
        lax.fori_loop(cuts[b], cuts[b + 1], slopes, 0)
        for k in range(n_layer - 1):
            block = parts.at[layer, pl.ds(cuts[b], cuts[b + 1] - cuts[b])]
            sum_copies.append(send(block, block, ss_sem.at[k, b], sr_sem.at[k, b], peers[k]))
    for copy in sum_copies:
        copy.wait_recv()
    whole = parts[0]
    for k in range(1, n_layer):
        whole = whole + parts[k]
    out[0] = whole[:, :, :half]
    out[1] = whole[:, :, half:]

    for copy in edge_copies + mid_copies + col_copies + sum_copies:
        copy.wait_send()


def on_device(sizes, layers, wind, offsets, weights, sub_index):
    rows, cols = sub_index.shape
    tiles = cols // LANES
    groups = rows // SUB
    wide = groups + 2 * FOOT // SUB
    smem = pl.BlockSpec(memory_space=pltpu.SMEM)
    hbm = pl.BlockSpec(memory_space=pltpu.HBM)
    return pl.pallas_call(
        functools.partial(kernel, sizes),
        out_shape=jax.ShapeDtypeStruct((2, DIRS, groups, cols // SUB), jnp.float32),
        in_specs=[smem, smem, hbm, hbm, hbm],
        out_specs=pl.BlockSpec(memory_space=pltpu.VMEM),
        scratch_shapes=[
            pltpu.VMEM((tiles + 2, rows + 2 * RIM, LANES), jnp.float32),
            pltpu.VMEM((tiles + 2, SUB, wide, LANES), jnp.float32),
            pltpu.VMEM(weights.shape, weights.dtype),
            pltpu.VMEM((DIRS, 2, tiles, rows, LANES), jnp.float32),
            pltpu.VMEM(sub_index.shape, sub_index.dtype),
            pltpu.VMEM((sizes[0], DIRS, groups, LANES), jnp.float32),
            pltpu.SemaphoreType.DMA((tiles + 2,)),
            pltpu.SemaphoreType.DMA((tiles, 2)),
            pltpu.SemaphoreType.DMA((tiles, 2)),
            pltpu.SemaphoreType.DMA((2, 3)),
            pltpu.SemaphoreType.DMA((2, 3)),
            pltpu.SemaphoreType.DMA((sizes[0] - 1, 3)),
            pltpu.SemaphoreType.DMA((sizes[0] - 1, 3)),
        ],
        compiler_params=pltpu.CompilerParams(
            collective_id=0, has_side_effects=True, vmem_limit_bytes=60 * 1024 * 1024
        ),
    )(wind, jnp.swapaxes(offsets, 1, 2), layers, weights, sub_index)


def solution(mesh):
    sizes = (mesh.shape["layer"], mesh.shape["tx"], mesh.shape["ty"])
    placed = (
        P("layer", "tx", "ty"),
        P("layer", None),
        P("layer", None, None),
        P(None, None, "tx", "ty"),
        P("tx", "ty"),
    )
    return jax.shard_map(
        functools.partial(on_device, sizes),
        mesh=mesh, in_specs=placed, out_specs=P(None, None, "tx", "ty"), check_vma=False,
    )
```

profile of v0, /device:TPU:0, one launch (start us, length us, event | category | flops | bytes accessed | tf_op | source)
XLA Modules:
  0.0 25.1 jit_solution(1144345501949570825)
XLA Ops:
  0.0 23.5 %shard_map.55 = f32[2,9,16,64]{3,2,1,0:T(8,128)} custom-call(s32[1,2]{1,0:T(1,128)} %wind.1, s32[1,2,9]{2,1,0:T(2,128)} %bitcast.1, f32[1,128,512]{2,1,0:T(8,128)} %layers.1, bf16[9,2,128,512]{3,2,1,0:T(8,128)(2,1)} %weights.1, s32[128,512]{1,0:T(8,128)} %sub_index.1), custom_call_target="tpu_custom_call" | custom-call | tf_op jit(solution)/shard_map/pallas_call | solution.py:215
  23.5 1.6 %copy.7 = f32[2,9,16,64]{3,2,1,0:T(8,128)} copy(f32[2,9,16,64]{3,2,1,0:T(8,128)} %shard_map.55) | data formatting | bytes 147456
where the time goes:
time: 25.2 us; the launch traced here: 25.1 us
  Pallas kernels  23.5 us (93%)
  local copies, waits for them, and re-layouts  1.58 us (6%)
    pallas_call x1, Pallas kernels, on_device(): pl.pallas_call(functools.partial(kernel, sizes), out_shape=jax.ShapeDtype...  23.5 us
    unnamed x1, local copies, waits for them, and re-layouts  1.58 us

commit v1 on v0

--- a/solution.py
+++ b/solution.py
@@ -17,7 +17,7 @@
 
 
 def kernel(
-    sizes, wind, offsets, layers, weights, sub_index, out, field, shifted, wraw, wlive, sub, parts,
+    sizes, wind_hbm, offsets_hbm, layers, weights, sub_index, out, wind, offsets, small_sem, field, shifted, wraw, wlive, sub, parts,
     local_sem, xs_sem, xr_sem, zs_sem, zr_sem, ss_sem, sr_sem,
 ):
     n_layer, n_tx, n_ty = sizes
@@ -35,6 +35,9 @@
     right = {"ty": lax.rem(ty + 1, n_ty)}
     peers = [{"layer": lax.rem(layer + k, n_layer)} for k in range(1, n_layer)]
 
+    small = [pltpu.make_async_copy(wind_hbm, wind, small_sem.at[0]), pltpu.make_async_copy(offsets_hbm, offsets, small_sem.at[1])]
+    for copy in small:
+        copy.start()
     order = [0, tiles - 1] + list(range(1, tiles - 1))
     own = {}
     for c in order:
@@ -99,6 +102,8 @@
 
     sub_copy.wait()
     weight_copy.wait()
+    for copy in small:
+        copy.wait()
 
     def prepare(d, carry):
         for c in range(tiles):
@@ -205,6 +210,10 @@
         copy.wait_send()
 
 
+def in_hbm(x):
+    return pltpu.with_memory_space_constraint(x, pltpu.HBM)
+
+
 def on_device(sizes, layers, wind, offsets, weights, sub_index):
     rows, cols = sub_index.shape
     tiles = cols // LANES
@@ -214,10 +223,13 @@
     hbm = pl.BlockSpec(memory_space=pltpu.HBM)
     return pl.pallas_call(
         functools.partial(kernel, sizes),
-        out_shape=jax.ShapeDtypeStruct((2, DIRS, groups, cols // SUB), jnp.float32),
-        in_specs=[smem, smem, hbm, hbm, hbm],
+        out_shape=pltpu.VMEM((2, DIRS, groups, cols // SUB), jnp.float32),
+        in_specs=[hbm, hbm, hbm, hbm, hbm],
         out_specs=pl.BlockSpec(memory_space=pltpu.VMEM),
         scratch_shapes=[
+            pltpu.SMEM((1, 2), jnp.int32),
+            pltpu.SMEM((1, 2, DIRS), jnp.int32),
+            pltpu.SemaphoreType.DMA((2,)),
             pltpu.VMEM((tiles + 2, rows + 2 * RIM, LANES), jnp.float32),
             pltpu.VMEM((tiles + 2, SUB, wide, LANES), jnp.float32),
             pltpu.VMEM(weights.shape, weights.dtype),
@@ -233,9 +245,9 @@
             pltpu.SemaphoreType.DMA((sizes[0] - 1, 3)),
         ],
         compiler_params=pltpu.CompilerParams(
-            collective_id=0, has_side_effects=True, vmem_limit_bytes=60 * 1024 * 1024
+            collective_id=0, has_side_effects=True, vmem_limit_bytes=32 * 1024 * 1024
         ),
-    )(wind, jnp.swapaxes(offsets, 1, 2), layers, weights, sub_index)
+    )(in_hbm(wind), in_hbm(jnp.swapaxes(offsets, 1, 2)), in_hbm(layers), in_hbm(weights), in_hbm(sub_index))
 
 
 def solution(mesh):

time: 25.2 us -> 23 us (0.913)
  Pallas kernels: 23.5 us -> 22.2 us
  local copies, waits for them, and re-layouts: 1.58 us -> 0.66 us
    pallas_call x1, Pallas kernels: 23.5 us -> 22.2 us  [on_device(): pl.pallas_call(functools.partial(kernel, sizes), out_shape=pltpu.VMEM((2,...]
    unnamed x1, local copies, waits for them, and re-layouts: 1.58 us -> 0.66 us
where the time goes in v1:
time: 23 us; the launch traced here: 22.8 us
  Pallas kernels  22.2 us (97%)
  local copies, waits for them, and re-layouts  0.66 us (3%)
    pallas_call x1, Pallas kernels, on_device(): pl.pallas_call(functools.partial(kernel, sizes), out_shape=pltpu.VMEM((2,...  22.2 us
    unnamed x1, local copies, waits for them, and re-layouts  0.66 us

profile of v1, /device:TPU:0, one launch (start us, length us, event | category | flops | bytes accessed | tf_op | source)
XLA Modules:
  0.0 22.8 jit_solution(16641225358549743625)
XLA Ops:
  0.0 22.2 %shard_map.55 = f32[2,9,16,64]{3,2,1,0:T(8,128)S(1)} custom-call(s32[1,2]{1,0:T(1,128)} %wind_hbm.1, s32[1,2,9]{2,1,0:T(2,128)} %bitcast.1, f32[1,128,512]{2,1,0:T(8,128)} %layers.1, bf16[9,2,128,512]{3,2,1,0:T(8,128)(2,1)} %weights.1, s32[128,512]{1,0:T(8,128)} %sub_index.1), custom_call_target="tpu_custom_call" | custom-call | tf_op jit(solution)/shard_map/pallas_call | solution.py:224
  22.2 0.7 %copy.7 = f32[2,9,16,64]{3,2,1,0:T(8,128)} copy(f32[2,9,16,64]{3,2,1,0:T(8,128)S(1)} %shard_map.55) | data formatting | bytes 147456

commit v2 on v1

v2 whole, which is shorter than its diff:
```python
import functools

import jax
import jax.numpy as jnp
from jax import lax
from jax.experimental import pallas as pl
from jax.experimental.pallas import tpu as pltpu
from jax.sharding import PartitionSpec as P

DIRS = 9
SUB = 8
LANES = 128
PAD = 72
MESH = pl.DeviceIdType.MESH
CUTS = (0, 3, 6, DIRS)
SPARE = 6


def kernel(
    sizes, wind_in, offsets_in, layers, weights, sub_index, out, wind, offsets, raw, wraw, sub, field, mixed,
    shifted, live, wlive, totals, parts, local_sem, zs_sem, zr_sem, xs_sem, xr_sem, cs_sem, cr_sem, ss_sem, sr_sem,
):
    n_layer, n_tx, n_ty = sizes
    rows, cols = sub_index.shape
    tiles = cols // LANES
    groups = rows // SUB
    wide = cols // SUB
    span = shifted.shape[1] // SUB
    layer = lax.axis_index("layer")
    tx = lax.axis_index("tx")
    ty = lax.axis_index("ty")
    up = {"tx": lax.rem(tx + n_tx - 1, n_tx)}
    down = {"tx": lax.rem(tx + 1, n_tx)}
    left = {"ty": lax.rem(ty + n_ty - 1, n_ty)}
    right = {"ty": lax.rem(ty + 1, n_ty)}
    peers = [{"layer": lax.rem(layer + k, n_layer)} for k in range(1, n_layer)]
    row_peers = [(down, 1)] if n_tx == 2 else [(down, 1), (up, 2)]
    col_peers = [(right, cols, 0), (left, PAD, PAD + cols)]

    order = [0, tiles - 1] + list(range(1, tiles - 1))
    own = {}
    for c in order:
        own[c] = pltpu.make_async_copy(layers.at[0, :, pl.ds(c * LANES, LANES)], raw.at[c], local_sem.at[c])
        own[c].start()
    local = [
        pltpu.make_async_copy(wind_in, wind, local_sem.at[tiles]),
        pltpu.make_async_copy(offsets_in, offsets, local_sem.at[tiles + 1]),
        pltpu.make_async_copy(sub_index, sub, local_sem.at[tiles + 2]),
        pltpu.make_async_copy(weights, wraw, local_sem.at[tiles + 3]),
    ]
    for copy in local:
        copy.start()

    barrier = pltpu.get_barrier_semaphore()
    greeted = [device for device, _ in row_peers] + [device for device, _, _ in col_peers] + peers
    greeted += [{**a, **b} for a, _ in row_peers for b, _, _ in col_peers]
    for device in greeted:
        pl.semaphore_signal(barrier, inc=1, device_id=device, device_id_type=MESH)

    for c in order:
        own[c].wait()
        field[0, pl.ds(PAD + c * LANES, LANES), :] = raw[c].T
    pl.semaphore_wait(barrier, len(greeted))

    def send(src, dst, send_sem, recv_sem, device):
        copy = pltpu.make_async_remote_copy(
            src_ref=src, dst_ref=dst, send_sem=send_sem, recv_sem=recv_sem,
            device_id=device, device_id_type=MESH,
        )
        copy.start()
        return copy

    side_copies, corner_copies = [], []
    for k, (b, start, end) in enumerate(col_peers):
        side_copies.append(send(
            field.at[0, pl.ds(start, PAD), :], field.at[0, pl.ds(end, PAD), :], zs_sem.at[k], zr_sem.at[k], b,
        ))
    for j, (a, slot) in enumerate(row_peers):
        for k, (b, start, end) in enumerate(col_peers):
            corner_copies.append(send(
                field.at[0, pl.ds(start, PAD), :], field.at[slot, pl.ds(end, PAD), :],
                cs_sem.at[j, k], cr_sem.at[j, k], {**a, **b},
            ))
    row_copies = [[
        send(
            field.at[0, pl.ds(PAD + c * LANES, LANES), :], field.at[slot, pl.ds(PAD + c * LANES, LANES), :],
            xs_sem.at[j, c], xr_sem.at[j, c], a,
        ) for j, (a, slot) in enumerate(row_peers)
    ] for c in range(tiles)]

    for copy in local:
        copy.wait()
    qrow = lax.shift_right_arithmetic(wind[0, 0], 6)
    qcol = lax.shift_right_arithmetic(wind[0, 1], 6)
    frow = (wind[0, 0] - 64 * qrow).astype(jnp.float32) / 64.0
    fcol = (wind[0, 1] - 64 * qcol).astype(jnp.float32) / 64.0

    for c in range(tiles):
        live[pl.ds(c * LANES, LANES), :] = (sub[:, pl.ds(c * LANES, LANES)] >= 0).astype(jnp.float32).T

    def prepare(d, carry):
        turn = (offsets[0, 0, d] - qrow) & (LANES - 1)
        for s in range(2):
            for c in range(tiles):
                w = wraw[d, s, :, pl.ds(c * LANES, LANES)].astype(jnp.float32).T
                w = pltpu.roll(w * live[pl.ds(c * LANES, LANES), :], turn, 1)
                for g in range(LANES // SUB):
                    wlive[d, s, pl.ds(c * (LANES // SUB) + g, SUB, stride=wide), :] = w[g * SUB : (g + 1) * SUB]
        return carry

    lax.fori_loop(0, DIRS, prepare, 0)

    def mix(start, size):
        lane = lax.broadcasted_iota(jnp.int32, (size, LANES), 1)
        here = [field[t, pl.ds(start, size), :] for t in range(len(row_peers) + 1)]
        turned = [pltpu.roll(h, 1, 1) for h in here]
        if n_tx == 2:
            before = [jnp.where(lane == 0, turned[1], turned[0]), jnp.where(lane == 0, turned[0], turned[1])]
        else:
            before = [
                jnp.where(lane == 0, turned[1], turned[0]), turned[1], jnp.where(lane == 0, turned[0], turned[2]),
            ]
        for t, (h, b) in enumerate(zip(here, before)):
            mixed[t, pl.ds(SUB + start, size), :] = (1.0 - frow) * h + frow * b
        for t in range(len(here)):
            for g in range(size // SUB):
                one = mixed[t, pl.ds(SUB + start + g * SUB, SUB), :]
                two = mixed[t, pl.ds(SUB - 1 + start + g * SUB, SUB), :]
                shifted[t, pl.ds(start // SUB + g, SUB, stride=span), :] = (1.0 - fcol) * one + fcol * two

    for t in range(len(row_peers) + 1):
        mixed[t, pl.ds(0, SUB), :] = jnp.zeros((SUB, LANES), jnp.float32)
    for copy in side_copies + corner_copies:
        copy.wait_recv()
    mix(0, PAD)
    for c in range(tiles):
        for copy in row_copies[c]:
            copy.wait_recv()
        mix(PAD + c * LANES, LANES)
    mix(PAD + cols, PAD)

    lane_w = lax.broadcasted_iota(jnp.int32, (wide, LANES), 1)
    pick_row = lax.broadcasted_iota(jnp.int32, (groups, 2 * LANES), 0)
    pick_col = lax.broadcasted_iota(jnp.int32, (groups, 2 * LANES), 1)

    def slopes(d, carry):
        turn = offsets[0, 0, d] - qrow
        top = offsets[0, 1, d] - qcol + PAD
        inside = (lane_w >= turn) & (lane_w < LANES + turn)
        sums = [None, None]
        for r in range(SUB):
            start = ((top + r) & (SUB - 1)) * span + lax.shift_right_arithmetic(top + r, 3)
            seen = [shifted[t, pl.ds(start, wide), :] for t in range(len(row_peers) + 1)]
            other = seen[1] if n_tx == 2 else jnp.where(lane_w < turn, seen[2], seen[1])
            view = jnp.where(inside, seen[0], other)
            for s in range(2):
                term = wlive[d, s, pl.ds(r * wide, wide), :] * view
                sums[s] = term if r == 0 else sums[s] + term
        for s in range(2):
            high = sums[s].astype(jnp.bfloat16)
            totals[d, pl.ds(s * wide, wide), pl.ds(0, LANES)] = high
            totals[d, pl.ds(s * wide, wide), pl.ds(LANES, LANES)] = (
                sums[s] - high.astype(jnp.float32)
            ).astype(jnp.bfloat16)
        return carry

    def gather(d, carry):
        turn = offsets[0, 0, d] - qrow
        pick = (lax.shift_right_logical((pick_col - turn) & (LANES - 1), 3) == pick_row).astype(jnp.bfloat16)
        parts[layer, d, :, :] = lax.dot_general(
            pick, totals[d], (((1,), (1,)), ((), ())), preferred_element_type=jnp.float32
        )
        return carry

    sum_copies = []
    for b in range(len(CUTS) - 1):
        lax.fori_loop(CUTS[b], CUTS[b + 1], slopes, 0)
        for d in range(CUTS[b], CUTS[b + 1]):
            gather(d, 0)
        for k in range(n_layer - 1):
            block = parts.at[layer, pl.ds(CUTS[b], CUTS[b + 1] - CUTS[b])]
            sum_copies.append(send(block, block, ss_sem.at[k, b], sr_sem.at[k, b], peers[k]))
    for copy in sum_copies:
        copy.wait_recv()
    whole = parts[0]
    for k in range(1, n_layer):
        whole = whole + parts[k]
    out[0] = whole[:, :, :wide]
    out[1] = whole[:, :, wide:]

    for copy in side_copies + corner_copies + sum(row_copies, []) + sum_copies:
        copy.wait_send()


def in_hbm(x):
    return pltpu.with_memory_space_constraint(x, pltpu.HBM)


def on_device(sizes, layers, wind, offsets, weights, sub_index):
    rows, cols = sub_index.shape
    tiles = cols // LANES
    groups = rows // SUB
    wide = cols // SUB
    seen = 2 if sizes[1] == 2 else 3
    deep = cols + 2 * PAD
    hbm = pl.BlockSpec(memory_space=pltpu.HBM)
    dma = pltpu.SemaphoreType.DMA
    return pl.pallas_call(
        functools.partial(kernel, sizes),
        out_shape=pltpu.VMEM((2, DIRS, groups, wide), jnp.float32),
        in_specs=[hbm] * 5,
        out_specs=pl.BlockSpec(memory_space=pltpu.VMEM),
        scratch_shapes=[
            pltpu.SMEM((1, 2), jnp.int32),
            pltpu.SMEM((1, 2, DIRS), jnp.int32),
            pltpu.VMEM((tiles, rows, LANES), jnp.float32),
            pltpu.VMEM(weights.shape, weights.dtype),
            pltpu.VMEM(sub_index.shape, sub_index.dtype),
            pltpu.VMEM((seen, deep, LANES), jnp.float32),
            pltpu.VMEM((seen, deep + SUB, LANES), jnp.float32),
            pltpu.VMEM((seen, deep + SPARE * SUB, LANES), jnp.float32),
            pltpu.VMEM((cols, LANES), jnp.float32),
            pltpu.VMEM((DIRS, 2, cols, LANES), jnp.float32),
            pltpu.VMEM((DIRS, 2 * wide, 2 * LANES), jnp.bfloat16),
            pltpu.VMEM((sizes[0], DIRS, groups, LANES), jnp.float32),
            dma((tiles + 4,)),
            dma((2,)),
            dma((2,)),
            dma((seen - 1, tiles)),
            dma((seen - 1, tiles)),
            dma((seen - 1, 2)),
            dma((seen - 1, 2)),
            dma((sizes[0] - 1, len(CUTS) - 1)),
            dma((sizes[0] - 1, len(CUTS) - 1)),
        ],
        compiler_params=pltpu.CompilerParams(
            collective_id=0, has_side_effects=True, vmem_limit_bytes=32 * 1024 * 1024
        ),
    )(in_hbm(wind), in_hbm(jnp.swapaxes(offsets, 1, 2)), in_hbm(layers), in_hbm(weights), in_hbm(sub_index))


def solution(mesh):
    sizes = (mesh.shape["layer"], mesh.shape["tx"], mesh.shape["ty"])
    placed = (
        P("layer", "tx", "ty"),
        P("layer", None),
        P("layer", None, None),
        P(None, None, "tx", "ty"),
        P("tx", "ty"),
    )
    return jax.shard_map(
        functools.partial(on_device, sizes),
        mesh=mesh, in_specs=placed, out_specs=P(None, None, "tx", "ty"), check_vma=False,
    )
```

time: 23 us -> 20.3 us (0.88)
  Pallas kernels: 22.2 us -> 19.5 us
    pallas_call x1, Pallas kernels: 22.2 us -> 19.5 us  [on_device(): pl.pallas_call(functools.partial(kernel, sizes), out_shape=pltpu.VMEM((2,...]
where the time goes in v2:
time: 20.3 us; the launch traced here: 20.2 us
  Pallas kernels  19.5 us (96%)
  local copies, waits for them, and re-layouts  0.66 us (3%)
    pallas_call x1, Pallas kernels, on_device(): pl.pallas_call(functools.partial(kernel, sizes), out_shape=pltpu.VMEM((2,...  19.5 us
    unnamed x1, local copies, waits for them, and re-layouts  0.66 us

profile of v2, /device:TPU:0, one launch (start us, length us, event | category | flops | bytes accessed | tf_op | source)
XLA Modules:
  0.0 20.2 jit_solution(4979170419968752771)
XLA Ops:
  0.0 19.5 %shard_map.55 = f32[2,9,16,64]{3,2,1,0:T(8,128)S(1)} custom-call(s32[1,2]{1,0:T(1,128)} %wind_in.1, s32[1,2,9]{2,1,0:T(2,128)} %bitcast.1, f32[1,128,512]{2,1,0:T(8,128)} %layers.1, bf16[9,2,128,512]{3,2,1,0:T(8,128)(2,1)} %weights.1, s32[128,512]{1,0:T(8,128)} %sub_index.1), custom_call_target="tpu_custom_call" | custom-call | tf_op jit(solution)/shard_map/pallas_call | solution.py:208
  19.5 0.7 %copy.7 = f32[2,9,16,64]{3,2,1,0:T(8,128)} copy(f32[2,9,16,64]{3,2,1,0:T(8,128)S(1)} %shard_map.55) | data formatting | bytes 147456

commit v3 on v2

--- a/solution.py
+++ b/solution.py
@@ -12,7 +12,6 @@
 LANES = 128
 PAD = 72
 MESH = pl.DeviceIdType.MESH
-CUTS = (0, 3, 6, DIRS)
 SPARE = 6
 
 
@@ -36,6 +35,8 @@
     peers = [{"layer": lax.rem(layer + k, n_layer)} for k in range(1, n_layer)]
     row_peers = [(down, 1)] if n_tx == 2 else [(down, 1), (up, 2)]
     col_peers = [(right, cols, 0), (left, PAD, PAD + cols)]
+    ends = [PAD + min((c + 1) * LANES + PAD, cols) for c in range(tiles)]
+    chunks = list(zip([PAD] + ends[:-1], ends))
 
     order = [0, tiles - 1] + list(range(1, tiles - 1))
     own = {}
@@ -83,10 +84,10 @@
             ))
     row_copies = [[
         send(
-            field.at[0, pl.ds(PAD + c * LANES, LANES), :], field.at[slot, pl.ds(PAD + c * LANES, LANES), :],
+            field.at[0, pl.ds(start, end - start), :], field.at[slot, pl.ds(start, end - start), :],
             xs_sem.at[j, c], xr_sem.at[j, c], a,
         ) for j, (a, slot) in enumerate(row_peers)
-    ] for c in range(tiles)]
+    ] for c, (start, end) in enumerate(chunks)]
 
     for copy in local:
         copy.wait()
@@ -111,6 +112,11 @@
     lax.fori_loop(0, DIRS, prepare, 0)
 
     def mix(start, size):
+        for at in range(start, start + size, SUB):
+            mix_group(at)
+
+    def mix_group(start):
+        size = SUB
         lane = lax.broadcasted_iota(jnp.int32, (size, LANES), 1)
         here = [field[t, pl.ds(start, size), :] for t in range(len(row_peers) + 1)]
         turned = [pltpu.roll(h, 1, 1) for h in here]
@@ -128,67 +134,86 @@
                 two = mixed[t, pl.ds(SUB - 1 + start + g * SUB, SUB), :]
                 shifted[t, pl.ds(start // SUB + g, SUB, stride=span), :] = (1.0 - fcol) * one + fcol * two
 
-    for t in range(len(row_peers) + 1):
-        mixed[t, pl.ds(0, SUB), :] = jnp.zeros((SUB, LANES), jnp.float32)
-    for copy in side_copies + corner_copies:
-        copy.wait_recv()
-    mix(0, PAD)
-    for c in range(tiles):
-        for copy in row_copies[c]:
-            copy.wait_recv()
-        mix(PAD + c * LANES, LANES)
-    mix(PAD + cols, PAD)
-
-    lane_w = lax.broadcasted_iota(jnp.int32, (wide, LANES), 1)
+    part = LANES // SUB
+    lane_w = lax.broadcasted_iota(jnp.int32, (part, LANES), 1)
     pick_row = lax.broadcasted_iota(jnp.int32, (groups, 2 * LANES), 0)
     pick_col = lax.broadcasted_iota(jnp.int32, (groups, 2 * LANES), 1)
-
-    def slopes(d, carry):
+    pick = (lax.shift_right_logical(pick_col & (LANES - 1), 3) == pick_row).astype(jnp.bfloat16)
+
+    def slopes(c, d):
         turn = offsets[0, 0, d] - qrow
         top = offsets[0, 1, d] - qcol + PAD
         inside = (lane_w >= turn) & (lane_w < LANES + turn)
         sums = [None, None]
         for r in range(SUB):
-            start = ((top + r) & (SUB - 1)) * span + lax.shift_right_arithmetic(top + r, 3)
-            seen = [shifted[t, pl.ds(start, wide), :] for t in range(len(row_peers) + 1)]
+            start = ((top + r) & (SUB - 1)) * span + lax.shift_right_arithmetic(top + r, 3) + c * part
+            seen = [shifted[t, pl.ds(start, part), :] for t in range(len(row_peers) + 1)]
             other = seen[1] if n_tx == 2 else jnp.where(lane_w < turn, seen[2], seen[1])
             view = jnp.where(inside, seen[0], other)
             for s in range(2):
-                term = wlive[d, s, pl.ds(r * wide, wide), :] * view
+                term = wlive[d, s, pl.ds(r * wide + c * part, part), :] * view
                 sums[s] = term if r == 0 else sums[s] + term
         for s in range(2):
-            high = sums[s].astype(jnp.bfloat16)
-            totals[d, pl.ds(s * wide, wide), pl.ds(0, LANES)] = high
-            totals[d, pl.ds(s * wide, wide), pl.ds(LANES, LANES)] = (
-                sums[s] - high.astype(jnp.float32)
-            ).astype(jnp.bfloat16)
+            item = 2 * d + s
+            place = (item & ~(SUB - 1)) + ((item + c) & (SUB - 1))
+            back = pltpu.roll(sums[s], (-turn) & (LANES - 1), 1)
+            high = back.astype(jnp.bfloat16)
+            low = (back - high.astype(jnp.float32)).astype(jnp.bfloat16)
+            at = pl.ds(pl.multiple_of(place * part, part), part)
+            totals[c, at, pl.ds(0, LANES)] = high
+            totals[c, at, pl.ds(LANES, LANES)] = low
+
+    def three(c, i, carry):
+        for k in range(3):
+            slopes(c, 3 * i + k)
         return carry
 
-    def gather(d, carry):
-        turn = offsets[0, 0, d] - qrow
-        pick = (lax.shift_right_logical((pick_col - turn) & (LANES - 1), 3) == pick_row).astype(jnp.bfloat16)
-        parts[layer, d, :, :] = lax.dot_general(
-            pick, totals[d], (((1,), (1,)), ((), ())), preferred_element_type=jnp.float32
+    totals[...] = jnp.zeros_like(totals)
+    for t in range(len(row_peers) + 1):
+        mixed[t, pl.ds(0, SUB), :] = jnp.zeros((SUB, LANES), jnp.float32)
+    sum_copies = []
+    for c in range(tiles):
+        if c == 0:
+            for copy in side_copies + corner_copies:
+                copy.wait_recv()
+            mix(0, PAD)
+        for copy in row_copies[c]:
+            copy.wait_recv()
+        mix(chunks[c][0], chunks[c][1] - chunks[c][0])
+        if c == tiles - 1:
+            mix(PAD + cols, PAD)
+        lax.fori_loop(0, DIRS // 3, functools.partial(three, c), 0)
+        parts[layer, c, :, :] = lax.dot_general(
+            pick, totals[c], (((1,), (1,)), ((), ())), preferred_element_type=jnp.float32
         )
-        return carry
-
-    sum_copies = []
-    for b in range(len(CUTS) - 1):
-        lax.fori_loop(CUTS[b], CUTS[b + 1], slopes, 0)
-        for d in range(CUTS[b], CUTS[b + 1]):
-            gather(d, 0)
-        for k in range(n_layer - 1):
-            block = parts.at[layer, pl.ds(CUTS[b], CUTS[b + 1] - CUTS[b])]
-            sum_copies.append(send(block, block, ss_sem.at[k, b], sr_sem.at[k, b], peers[k]))
-    for copy in sum_copies:
-        copy.wait_recv()
-    whole = parts[0]
-    for k in range(1, n_layer):
-        whole = whole + parts[k]
-    out[0] = whole[:, :, :wide]
-    out[1] = whole[:, :, wide:]
-
-    for copy in side_copies + corner_copies + sum(row_copies, []) + sum_copies:
+        block = parts.at[layer, c]
+        sum_copies.append([
+            send(block, block, ss_sem.at[k, c], sr_sem.at[k, c], peers[k]) for k in range(n_layer - 1)
+        ])
+    whole = []
+    for c in range(tiles):
+        for copy in sum_copies[c]:
+            copy.wait_recv()
+        total = parts[0, c]
+        for k in range(1, n_layer):
+            total = total + parts[k, c]
+        whole.append(total)
+    lane_g = lax.broadcasted_iota(jnp.int32, (groups, LANES), 1)
+    for d in range(DIRS):
+        for s in range(2):
+            item = 2 * d + s
+            first = item & (SUB - 1)
+            block = None
+            for c in range(tiles):
+                slot = (first + c) & (SUB - 1)
+                piece = whole[c][:, item // SUB * LANES : (item // SUB + 1) * LANES]
+                inside = (lane_g >= slot * part) & (lane_g < (slot + 1) * part)
+                block = piece if block is None else jnp.where(inside, piece, block)
+            if first:
+                block = pltpu.roll(block, LANES - first * part, 1)
+            out[s, d] = block[:, :wide]
+
+    for copy in side_copies + corner_copies + sum(row_copies, []) + sum(sum_copies, []):
         copy.wait_send()
 
 
@@ -203,6 +228,7 @@
     wide = cols // SUB
     seen = 2 if sizes[1] == 2 else 3
     deep = cols + 2 * PAD
+    deep_out = -(-2 * DIRS // SUB) * LANES
     hbm = pl.BlockSpec(memory_space=pltpu.HBM)
     dma = pltpu.SemaphoreType.DMA
     return pl.pallas_call(
@@ -221,8 +247,8 @@
             pltpu.VMEM((seen, deep + SPARE * SUB, LANES), jnp.float32),
             pltpu.VMEM((cols, LANES), jnp.float32),
             pltpu.VMEM((DIRS, 2, cols, LANES), jnp.float32),
-            pltpu.VMEM((DIRS, 2 * wide, 2 * LANES), jnp.bfloat16),
-            pltpu.VMEM((sizes[0], DIRS, groups, LANES), jnp.float32),
+            pltpu.VMEM((tiles, deep_out, 2 * LANES), jnp.bfloat16),
+            pltpu.VMEM((sizes[0], tiles, groups, deep_out), jnp.float32),
             dma((tiles + 4,)),
             dma((2,)),
             dma((2,)),
@@ -230,8 +256,8 @@
             dma((seen - 1, tiles)),
             dma((seen - 1, 2)),
             dma((seen - 1, 2)),
-            dma((sizes[0] - 1, len(CUTS) - 1)),
-            dma((sizes[0] - 1, len(CUTS) - 1)),
+            dma((sizes[0] - 1, tiles)),
+            dma((sizes[0] - 1, tiles)),
         ],
         compiler_params=pltpu.CompilerParams(
             collective_id=0, has_side_effects=True, vmem_limit_bytes=32 * 1024 * 1024

time: 20.3 us -> 19.6 us (0.966)
  Pallas kernels: 19.5 us -> 18.8 us
    pallas_call x1, Pallas kernels: 19.5 us -> 18.8 us  [on_device(): pl.pallas_call(functools.partial(kernel, sizes), out_shape=pltpu.VMEM((2,...]
where the time goes in v3:
time: 19.6 us; the launch traced here: 19.4 us
  Pallas kernels  18.8 us (96%)
  local copies, waits for them, and re-layouts  0.66 us (3%)
    pallas_call x1, Pallas kernels, on_device(): pl.pallas_call(functools.partial(kernel, sizes), out_shape=pltpu.VMEM((2,...  18.8 us
    unnamed x1, local copies, waits for them, and re-layouts  0.66 us

profile of v3, /device:TPU:0, one launch (start us, length us, event | category | flops | bytes accessed | tf_op | source)
XLA Modules:
  0.0 19.4 jit_solution(5744982249415714309)
XLA Ops:
  0.0 18.8 %shard_map.55 = f32[2,9,16,64]{3,2,1,0:T(8,128)S(1)} custom-call(s32[1,2]{1,0:T(1,128)} %wind_in.1, s32[1,2,9]{2,1,0:T(2,128)} %bitcast.1, f32[1,128,512]{2,1,0:T(8,128)} %layers.1, bf16[9,2,128,512]{3,2,1,0:T(8,128)(2,1)} %weights.1, s32[128,512]{1,0:T(8,128)} %sub_index.1), custom_call_target="tpu_custom_call" | custom-call | tf_op jit(solution)/shard_map/pallas_call | solution.py:234
  18.8 0.7 %copy.7 = f32[2,9,16,64]{3,2,1,0:T(8,128)} copy(f32[2,9,16,64]{3,2,1,0:T(8,128)S(1)} %shard_map.55) | data formatting | bytes 147456

commit v4 on v3

--- a/solution.py
+++ b/solution.py
@@ -17,7 +17,7 @@
 
 def kernel(
     sizes, wind_in, offsets_in, layers, weights, sub_index, out, wind, offsets, raw, wraw, sub, field, mixed,
-    shifted, live, wlive, totals, parts, local_sem, zs_sem, zr_sem, xs_sem, xr_sem, cs_sem, cr_sem, ss_sem, sr_sem,
+    shifted, live, wlive, totals, parts, local_sem, zs_sem, zr_sem, xs_sem, xr_sem, cs_sem, cr_sem, ss_sem, sr_sem, ready,
 ):
     n_layer, n_tx, n_ty = sizes
     rows, cols = sub_index.shape
@@ -35,8 +35,9 @@
     peers = [{"layer": lax.rem(layer + k, n_layer)} for k in range(1, n_layer)]
     row_peers = [(down, 1)] if n_tx == 2 else [(down, 1), (up, 2)]
     col_peers = [(right, cols, 0), (left, PAD, PAD + cols)]
-    ends = [PAD + min((c + 1) * LANES + PAD, cols) for c in range(tiles)]
-    chunks = list(zip([PAD] + ends[:-1], ends))
+    stages = list(range(1, tiles - 1)) + [0, tiles - 1]
+    cut = [PAD + LANES - PAD] + [PAD + (c + 1) * LANES + PAD for c in range(1, tiles - 1)]
+    chunks = list(zip(cut[:-1], cut[1:])) + [(PAD, cut[0]), (cut[-1], PAD + cols)]
 
     order = [0, tiles - 1] + list(range(1, tiles - 1))
     own = {}
@@ -53,35 +54,69 @@
         copy.start()
 
     barrier = pltpu.get_barrier_semaphore()
-    greeted = [device for device, _ in row_peers] + [device for device, _, _ in col_peers] + peers
-    greeted += [{**a, **b} for a, _ in row_peers for b, _, _ in col_peers]
-    for device in greeted:
-        pl.semaphore_signal(barrier, inc=1, device_id=device, device_id_type=MESH)
+    def signal(semaphore, devices):
+        for device in devices:
+            pl.semaphore_signal(semaphore, inc=1, device_id=device, device_id_type=MESH)
+
+    at_right = [right] + [{**a, **right} for a, _ in row_peers]
+    at_left = [left] + [{**a, **left} for a, _ in row_peers]
+    same = [device for device, _ in row_peers] + peers
+    ahead_right = ty != 0
+    ahead_left = ty == 1
+    signal(barrier, same)
+
+    @pl.when(ty != 1)
+    def _():
+        signal(barrier, at_left)
+
+    @pl.when(ty == 0)
+    def _():
+        signal(barrier, at_right)
 
     for c in order:
         own[c].wait()
         field[0, pl.ds(PAD + c * LANES, LANES), :] = raw[c].T
-    pl.semaphore_wait(barrier, len(greeted))
-
-    def send(src, dst, send_sem, recv_sem, device):
-        copy = pltpu.make_async_remote_copy(
+    pl.semaphore_wait(
+        barrier,
+        len(same) + len(at_right) * ahead_right.astype(jnp.int32) + len(at_left) * ahead_left.astype(jnp.int32),
+    )
+
+    def plan(src, dst, send_sem, recv_sem, device):
+        return pltpu.make_async_remote_copy(
             src_ref=src, dst_ref=dst, send_sem=send_sem, recv_sem=recv_sem,
             device_id=device, device_id_type=MESH,
         )
+
+    def send(*args):
+        copy = plan(*args)
         copy.start()
         return copy
 
-    side_copies, corner_copies = [], []
+    col_copies = [[], []]
     for k, (b, start, end) in enumerate(col_peers):
-        side_copies.append(send(
+        col_copies[k].append(plan(
             field.at[0, pl.ds(start, PAD), :], field.at[0, pl.ds(end, PAD), :], zs_sem.at[k], zr_sem.at[k], b,
         ))
-    for j, (a, slot) in enumerate(row_peers):
-        for k, (b, start, end) in enumerate(col_peers):
-            corner_copies.append(send(
+        for j, (a, slot) in enumerate(row_peers):
+            col_copies[k].append(plan(
                 field.at[0, pl.ds(start, PAD), :], field.at[slot, pl.ds(end, PAD), :],
                 cs_sem.at[j, k], cr_sem.at[j, k], {**a, **b},
             ))
+
+    def start_all(copies):
+        for copy in copies:
+            copy.start()
+
+    @pl.when(ahead_right)
+    def _():
+        signal(ready, at_right)
+        start_all(col_copies[0])
+
+    @pl.when(ahead_left)
+    def _():
+        signal(ready, at_left)
+        start_all(col_copies[1])
+
     row_copies = [[
         send(
             field.at[0, pl.ds(start, end - start), :], field.at[slot, pl.ds(start, end - start), :],
@@ -96,20 +131,35 @@
     frow = (wind[0, 0] - 64 * qrow).astype(jnp.float32) / 64.0
     fcol = (wind[0, 1] - 64 * qcol).astype(jnp.float32) / 64.0
 
-    for c in range(tiles):
-        live[pl.ds(c * LANES, LANES), :] = (sub[:, pl.ds(c * LANES, LANES)] >= 0).astype(jnp.float32).T
-
-    def prepare(d, carry):
-        turn = (offsets[0, 0, d] - qrow) & (LANES - 1)
-        for s in range(2):
-            for c in range(tiles):
-                w = wraw[d, s, :, pl.ds(c * LANES, LANES)].astype(jnp.float32).T
+    def prepare(c, i, carry):
+        for k in range(3):
+            d = 3 * i + k
+            turn = (offsets[0, 0, d] - qrow) & (LANES - 1)
+            for s in range(2):
+                w = wraw[d, s, :, pl.ds(c * LANES, LANES)].T.astype(jnp.float32)
                 w = pltpu.roll(w * live[pl.ds(c * LANES, LANES), :], turn, 1)
                 for g in range(LANES // SUB):
                     wlive[d, s, pl.ds(c * (LANES // SUB) + g, SUB, stride=wide), :] = w[g * SUB : (g + 1) * SUB]
         return carry
 
-    lax.fori_loop(0, DIRS, prepare, 0)
+    def prepare_all(c):
+        live[pl.ds(c * LANES, LANES), :] = (sub[:, pl.ds(c * LANES, LANES)] >= 0).astype(jnp.float32).T
+        lax.fori_loop(0, DIRS // 3, functools.partial(prepare, c), 0)
+
+    for c in stages[:2]:
+        prepare_all(c)
+
+    @pl.when(ty != 1)
+    def _():
+        pl.semaphore_wait(ready, len(at_left) + len(at_right) * (ty == 0).astype(jnp.int32))
+        start_all(col_copies[1])
+
+    @pl.when(ty == 0)
+    def _():
+        start_all(col_copies[0])
+
+    for c in stages[2:]:
+        prepare_all(c)
 
     def mix(start, size):
         for at in range(start, start + size, SUB):
@@ -155,51 +205,58 @@
                 sums[s] = term if r == 0 else sums[s] + term
         for s in range(2):
             item = 2 * d + s
-            place = (item & ~(SUB - 1)) + ((item + c) & (SUB - 1))
+            place = 2 * SUB * stages.index(c) + (item & SUB) + ((item + c) & (SUB - 1))
+            place = jnp.where(d == DIRS - 1, 2 * SUB * tiles + s * tiles + c, place)
             back = pltpu.roll(sums[s], (-turn) & (LANES - 1), 1)
             high = back.astype(jnp.bfloat16)
             low = (back - high.astype(jnp.float32)).astype(jnp.bfloat16)
             at = pl.ds(pl.multiple_of(place * part, part), part)
-            totals[c, at, pl.ds(0, LANES)] = high
-            totals[c, at, pl.ds(LANES, LANES)] = low
+            totals[at, pl.ds(0, LANES)] = high
+            totals[at, pl.ds(LANES, LANES)] = low
 
     def three(c, i, carry):
         for k in range(3):
             slopes(c, 3 * i + k)
         return carry
 
-    totals[...] = jnp.zeros_like(totals)
     for t in range(len(row_peers) + 1):
         mixed[t, pl.ds(0, SUB), :] = jnp.zeros((SUB, LANES), jnp.float32)
+    lines = [(2 * LANES * i, 2 * LANES) for i in range(tiles - 1)] + [(2 * LANES * (tiles - 1), 3 * LANES)]
     sum_copies = []
-    for c in range(tiles):
+    for i, c in enumerate(stages):
+        for copy in row_copies[i]:
+            copy.wait_recv()
         if c == 0:
-            for copy in side_copies + corner_copies:
+            for copy in col_copies[0]:
                 copy.wait_recv()
             mix(0, PAD)
-        for copy in row_copies[c]:
-            copy.wait_recv()
-        mix(chunks[c][0], chunks[c][1] - chunks[c][0])
+        mix(chunks[i][0], chunks[i][1] - chunks[i][0])
+        if c == 0:
+            mix(chunks[0][0], SUB)
         if c == tiles - 1:
+            for copy in col_copies[1]:
+                copy.wait_recv()
             mix(PAD + cols, PAD)
         lax.fori_loop(0, DIRS // 3, functools.partial(three, c), 0)
-        parts[layer, c, :, :] = lax.dot_general(
-            pick, totals[c], (((1,), (1,)), ((), ())), preferred_element_type=jnp.float32
+        line = pl.ds(*lines[i])
+        parts[layer, :, line] = lax.dot_general(
+            pick, totals[line, :], (((1,), (1,)), ((), ())), preferred_element_type=jnp.float32
         )
-        block = parts.at[layer, c]
+        block = parts.at[layer, :, line]
         sum_copies.append([
-            send(block, block, ss_sem.at[k, c], sr_sem.at[k, c], peers[k]) for k in range(n_layer - 1)
+            send(block, block, ss_sem.at[k, i], sr_sem.at[k, i], peers[k]) for k in range(n_layer - 1)
         ])
-    whole = []
-    for c in range(tiles):
-        for copy in sum_copies[c]:
+    whole = {}
+    for i, c in enumerate(stages):
+        for copy in sum_copies[i]:
             copy.wait_recv()
-        total = parts[0, c]
+        line = pl.ds(*lines[i])
+        total = parts[0, :, line]
         for k in range(1, n_layer):
-            total = total + parts[k, c]
-        whole.append(total)
+            total = total + parts[k, :, line]
+        whole[c] = total
     lane_g = lax.broadcasted_iota(jnp.int32, (groups, LANES), 1)
-    for d in range(DIRS):
+    for d in range(DIRS - 1):
         for s in range(2):
             item = 2 * d + s
             first = item & (SUB - 1)
@@ -212,8 +269,11 @@
             if first:
                 block = pltpu.roll(block, LANES - first * part, 1)
             out[s, d] = block[:, :wide]
-
-    for copy in side_copies + corner_copies + sum(row_copies, []) + sum(sum_copies, []):
+    block = whole[tiles - 1][:, 2 * LANES :]
+    out[0, DIRS - 1] = block[:, :wide]
+    out[1, DIRS - 1] = block[:, wide:]
+
+    for copy in col_copies[0] + col_copies[1] + sum(row_copies, []) + sum(sum_copies, []):
         copy.wait_send()
 
 
@@ -228,7 +288,7 @@
     wide = cols // SUB
     seen = 2 if sizes[1] == 2 else 3
     deep = cols + 2 * PAD
-    deep_out = -(-2 * DIRS // SUB) * LANES
+    deep_out = (2 * tiles + 1) * LANES
     hbm = pl.BlockSpec(memory_space=pltpu.HBM)
     dma = pltpu.SemaphoreType.DMA
     return pl.pallas_call(
@@ -247,8 +307,8 @@
             pltpu.VMEM((seen, deep + SPARE * SUB, LANES), jnp.float32),
             pltpu.VMEM((cols, LANES), jnp.float32),
             pltpu.VMEM((DIRS, 2, cols, LANES), jnp.float32),
-            pltpu.VMEM((tiles, deep_out, 2 * LANES), jnp.bfloat16),
-            pltpu.VMEM((sizes[0], tiles, groups, deep_out), jnp.float32),
+            pltpu.VMEM((deep_out, 2 * LANES), jnp.bfloat16),
+            pltpu.VMEM((sizes[0], groups, deep_out), jnp.float32),
             dma((tiles + 4,)),
             dma((2,)),
             dma((2,)),
@@ -258,6 +318,7 @@
             dma((seen - 1, 2)),
             dma((sizes[0] - 1, tiles)),
             dma((sizes[0] - 1, tiles)),
+            pltpu.SemaphoreType.REGULAR,
         ],
         compiler_params=pltpu.CompilerParams(
             collective_id=0, has_side_effects=True, vmem_limit_bytes=32 * 1024 * 1024

time: 19.6 us -> 18.4 us (0.939)
  Pallas kernels: 18.8 us -> 17.5 us
    pallas_call x1, Pallas kernels: 18.8 us -> 17.5 us  [on_device(): pl.pallas_call(functools.partial(kernel, sizes), out_shape=pltpu.VMEM((2,...]
where the time goes in v4:
time: 18.4 us; the launch traced here: 18.2 us
  Pallas kernels  17.5 us (95%)
  local copies, waits for them, and re-layouts  0.66 us (4%)
    pallas_call x1, Pallas kernels, on_device(): pl.pallas_call(functools.partial(kernel, sizes), out_shape=pltpu.VMEM((2,...  17.5 us
    unnamed x1, local copies, waits for them, and re-layouts  0.66 us

profile of v4, /device:TPU:0, one launch (start us, length us, event | category | flops | bytes accessed | tf_op | source)
XLA Modules:
  0.0 18.2 jit_solution(17831639017036926212)
XLA Ops:
  0.0 17.5 %shard_map.55 = f32[2,9,16,64]{3,2,1,0:T(8,128)S(1)} custom-call(s32[1,2]{1,0:T(1,128)} %wind_in.1, s32[1,2,9]{2,1,0:T(2,128)} %bitcast.1, f32[1,128,512]{2,1,0:T(8,128)} %layers.1, bf16[9,2,128,512]{3,2,1,0:T(8,128)(2,1)} %weights.1, s32[128,512]{1,0:T(8,128)} %sub_index.1), custom_call_target="tpu_custom_call" | custom-call | tf_op jit(solution)/shard_map/pallas_call | solution.py:294
  17.6 0.7 %copy.7 = f32[2,9,16,64]{3,2,1,0:T(8,128)} copy(f32[2,9,16,64]{3,2,1,0:T(8,128)S(1)} %shard_map.55) | data formatting | bytes 147456

commit v5 on v4

--- a/solution.py
+++ b/solution.py
@@ -32,12 +32,12 @@
     down = {"tx": lax.rem(tx + 1, n_tx)}
     left = {"ty": lax.rem(ty + n_ty - 1, n_ty)}
     right = {"ty": lax.rem(ty + 1, n_ty)}
-    peers = [{"layer": lax.rem(layer + k, n_layer)} for k in range(1, n_layer)]
+    peers = [{"layer": layer ^ k} for k in range(n_layer - 1, 0, -1)]
     row_peers = [(down, 1)] if n_tx == 2 else [(down, 1), (up, 2)]
     col_peers = [(right, cols, 0), (left, PAD, PAD + cols)]
-    stages = list(range(1, tiles - 1)) + [0, tiles - 1]
-    cut = [PAD + LANES - PAD] + [PAD + (c + 1) * LANES + PAD for c in range(1, tiles - 1)]
-    chunks = list(zip(cut[:-1], cut[1:])) + [(PAD, cut[0]), (cut[-1], PAD + cols)]
+    stages = [1, 0] + list(range(2, tiles))
+    cut = [PAD, 2 * PAD] + [PAD + (c + 1) * LANES + PAD for c in range(1, tiles - 1)] + [PAD + cols]
+    chunks = list(zip(cut[:-1], cut[1:]))
 
     order = [0, tiles - 1] + list(range(1, tiles - 1))
     own = {}
@@ -99,8 +99,8 @@
         ))
         for j, (a, slot) in enumerate(row_peers):
             col_copies[k].append(plan(
-                field.at[0, pl.ds(start, PAD), :], field.at[slot, pl.ds(end, PAD), :],
-                cs_sem.at[j, k], cr_sem.at[j, k], {**a, **b},
+                field.at[k * slot, pl.ds(start, PAD), :], field.at[slot, pl.ds(end, PAD), :],
+                cs_sem.at[j, k], cr_sem.at[j, k], b if k else {**a, **b},
             ))
 
     def start_all(copies):
@@ -109,13 +109,12 @@
 
     @pl.when(ahead_right)
     def _():
-        signal(ready, at_right)
+        signal(ready, [right])
         start_all(col_copies[0])
 
     @pl.when(ahead_left)
     def _():
         signal(ready, at_left)
-        start_all(col_copies[1])
 
     row_copies = [[
         send(
@@ -151,18 +150,21 @@
 
     @pl.when(ty != 1)
     def _():
-        pl.semaphore_wait(ready, len(at_left) + len(at_right) * (ty == 0).astype(jnp.int32))
-        start_all(col_copies[1])
+        pl.semaphore_wait(ready, 1 + len(at_right) * (ty == 0).astype(jnp.int32))
 
     @pl.when(ty == 0)
     def _():
         start_all(col_copies[0])
 
+    col_copies[1][0].start()
     for c in stages[2:]:
         prepare_all(c)
-
-    def mix(start, size):
-        for at in range(start, start + size, SUB):
+    for copy in row_copies[0]:
+        copy.wait_recv()
+    start_all(col_copies[1][1:])
+
+    def mix(start, end):
+        for at in range(start, end, SUB):
             mix_group(at)
 
     def mix_group(start):
@@ -206,11 +208,12 @@
         for s in range(2):
             item = 2 * d + s
             place = 2 * SUB * stages.index(c) + (item & SUB) + ((item + c) & (SUB - 1))
-            place = jnp.where(d == DIRS - 1, 2 * SUB * tiles + s * tiles + c, place)
+            if d == DIRS - 1:
+                place = 2 * SUB * tiles + s * tiles + c
             back = pltpu.roll(sums[s], (-turn) & (LANES - 1), 1)
             high = back.astype(jnp.bfloat16)
             low = (back - high.astype(jnp.float32)).astype(jnp.bfloat16)
-            at = pl.ds(pl.multiple_of(place * part, part), part)
+            at = pl.ds(place * part, part)
             totals[at, pl.ds(0, LANES)] = high
             totals[at, pl.ds(LANES, LANES)] = low
 
@@ -224,20 +227,23 @@
     lines = [(2 * LANES * i, 2 * LANES) for i in range(tiles - 1)] + [(2 * LANES * (tiles - 1), 3 * LANES)]
     sum_copies = []
     for i, c in enumerate(stages):
-        for copy in row_copies[i]:
-            copy.wait_recv()
+        if c:
+            for copy in row_copies[c]:
+                copy.wait_recv()
+        if c == 1:
+            mix(*chunks[0])
         if c == 0:
             for copy in col_copies[0]:
                 copy.wait_recv()
             mix(0, PAD)
-        mix(chunks[i][0], chunks[i][1] - chunks[i][0])
-        if c == 0:
-            mix(chunks[0][0], SUB)
+            mix(PAD, PAD + SUB)
+        else:
+            mix(*chunks[c])
         if c == tiles - 1:
             for copy in col_copies[1]:
                 copy.wait_recv()
-            mix(PAD + cols, PAD)
-        lax.fori_loop(0, DIRS // 3, functools.partial(three, c), 0)
+            mix(PAD + cols, 2 * PAD + cols)
+        [slopes(c, d) for d in range(DIRS)]
         line = pl.ds(*lines[i])
         parts[layer, :, line] = lax.dot_general(
             pick, totals[line, :], (((1,), (1,)), ((), ())), preferred_element_type=jnp.float32

time: 18.4 us -> 17.5 us (0.951)
  Pallas kernels: 17.5 us -> 16.7 us
    pallas_call x1, Pallas kernels: 17.5 us -> 16.7 us  [on_device(): pl.pallas_call(functools.partial(kernel, sizes), out_shape=pltpu.VMEM((2,...]
where the time goes in v5:
time: 17.5 us; the launch traced here: 17.3 us
  Pallas kernels  16.7 us (95%)
  local copies, waits for them, and re-layouts  0.66 us (4%)
    pallas_call x1, Pallas kernels, on_device(): pl.pallas_call(functools.partial(kernel, sizes), out_shape=pltpu.VMEM((2,...  16.7 us
    unnamed x1, local copies, waits for them, and re-layouts  0.66 us

profile of v5, /device:TPU:0, one launch (start us, length us, event | category | flops | bytes accessed | tf_op | source)
XLA Modules:
  0.0 17.3 jit_solution(7216050269164359434)
XLA Ops:
  0.0 16.7 %shard_map.55 = f32[2,9,16,64]{3,2,1,0:T(8,128)S(1)} custom-call(s32[1,2]{1,0:T(1,128)} %wind_in.1, s32[1,2,9]{2,1,0:T(2,128)} %bitcast.1, f32[1,128,512]{2,1,0:T(8,128)} %layers.1, bf16[9,2,128,512]{3,2,1,0:T(8,128)(2,1)} %weights.1, s32[128,512]{1,0:T(8,128)} %sub_index.1), custom_call_target="tpu_custom_call" | custom-call | tf_op jit(solution)/shard_map/pallas_call | solution.py:300
  16.7 0.7 %copy.7 = f32[2,9,16,64]{3,2,1,0:T(8,128)} copy(f32[2,9,16,64]{3,2,1,0:T(8,128)S(1)} %shard_map.55) | data formatting | bytes 147456

commit v6 on v5

--- a/solution.py
+++ b/solution.py
@@ -73,9 +73,11 @@
     def _():
         signal(barrier, at_right)
 
-    for c in order:
+    def turn_tile(c):
         own[c].wait()
         field[0, pl.ds(PAD + c * LANES, LANES), :] = raw[c].T
+
+    turn_tile(0)
     pl.semaphore_wait(
         barrier,
         len(same) + len(at_right) * ahead_right.astype(jnp.int32) + len(at_left) * ahead_left.astype(jnp.int32),
@@ -107,6 +109,18 @@
         for copy in copies:
             copy.start()
 
+    def send_rows(c):
+        start, end = chunks[c]
+        return [
+            send(
+                field.at[0, pl.ds(start, end - start), :], field.at[slot, pl.ds(start, end - start), :],
+                xs_sem.at[j, c], xr_sem.at[j, c], a,
+            ) for j, (a, slot) in enumerate(row_peers)
+        ]
+
+    row_copies = [send_rows(0)]
+    turn_tile(tiles - 1)
+
     @pl.when(ahead_right)
     def _():
         signal(ready, [right])
@@ -116,12 +130,12 @@
     def _():
         signal(ready, at_left)
 
-    row_copies = [[
-        send(
-            field.at[0, pl.ds(start, end - start), :], field.at[slot, pl.ds(start, end - start), :],
-            xs_sem.at[j, c], xr_sem.at[j, c], a,
-        ) for j, (a, slot) in enumerate(row_peers)
-    ] for c, (start, end) in enumerate(chunks)]
+    for c in range(1, tiles):
+        if c < tiles - 1:
+            for t in range(1 if c == 1 else c + 1, c + 2):
+                if t < tiles - 1:
+                    turn_tile(t)
+        row_copies.append(send_rows(c))
 
     for copy in local:
         copy.wait()
@@ -157,11 +171,12 @@
         start_all(col_copies[0])
 
     col_copies[1][0].start()
-    for c in stages[2:]:
+    for c in stages[2:-1]:
         prepare_all(c)
     for copy in row_copies[0]:
         copy.wait_recv()
     start_all(col_copies[1][1:])
+    prepare_all(stages[-1])
 
     def mix(start, end):
         for at in range(start, end, SUB):
@@ -243,15 +258,20 @@
             for copy in col_copies[1]:
                 copy.wait_recv()
             mix(PAD + cols, 2 * PAD + cols)
-        [slopes(c, d) for d in range(DIRS)]
-        line = pl.ds(*lines[i])
-        parts[layer, :, line] = lax.dot_general(
-            pick, totals[line, :], (((1,), (1,)), ((), ())), preferred_element_type=jnp.float32
-        )
-        block = parts.at[layer, :, line]
-        sum_copies.append([
-            send(block, block, ss_sem.at[k, i], sr_sem.at[k, i], peers[k]) for k in range(n_layer - 1)
-        ])
+        sum_copies.append([])
+        edges = [0, DIRS - 1] if i < tiles - 1 else [0, SUB // 2, DIRS - 1]
+        for n, (low, high) in enumerate(zip(edges[:-1], edges[1:])):
+            last = i == tiles - 1 and high == DIRS - 1
+            for d in range(low, high + 1 if last or i < tiles - 1 else high):
+                slopes(c, d)
+            line = pl.ds(2 * LANES * i + 2 * low // SUB * LANES, ((2 * high - 2 * low) // SUB + last) * LANES)
+            parts[layer, :, line] = lax.dot_general(
+                pick, totals[line, :], (((1,), (1,)), ((), ())), preferred_element_type=jnp.float32
+            )
+            block = parts.at[layer, :, line]
+            sum_copies[i] += [
+                send(block, block, ss_sem.at[k, i + n], sr_sem.at[k, i + n], peers[k]) for k in range(n_layer - 1)
+            ]
     whole = {}
     for i, c in enumerate(stages):
         for copy in sum_copies[i]:
@@ -322,8 +342,8 @@
             dma((seen - 1, tiles)),
             dma((seen - 1, 2)),
             dma((seen - 1, 2)),
-            dma((sizes[0] - 1, tiles)),
-            dma((sizes[0] - 1, tiles)),
+            dma((sizes[0] - 1, tiles + 1)),
+            dma((sizes[0] - 1, tiles + 1)),
             pltpu.SemaphoreType.REGULAR,
         ],
         compiler_params=pltpu.CompilerParams(

time: 17.5 us -> 17 us (0.971)
  Pallas kernels: 16.7 us -> 16.2 us
    pallas_call x1, Pallas kernels: 16.7 us -> 16.2 us  [on_device(): pl.pallas_call(functools.partial(kernel, sizes), out_shape=pltpu.VMEM((2,...]
where the time goes in v6:
time: 17 us; the launch traced here: 16.8 us
  Pallas kernels  16.2 us (95%)
  local copies, waits for them, and re-layouts  0.66 us (4%)
    pallas_call x1, Pallas kernels, on_device(): pl.pallas_call(functools.partial(kernel, sizes), out_shape=pltpu.VMEM((2,...  16.2 us
    unnamed x1, local copies, waits for them, and re-layouts  0.66 us

profile of v6, /device:TPU:0, one launch (start us, length us, event | category | flops | bytes accessed | tf_op | source)
XLA Modules:
  0.0 16.8 jit_solution(18018399689987326894)
XLA Ops:
  0.0 16.2 %shard_map.55 = f32[2,9,16,64]{3,2,1,0:T(8,128)S(1)} custom-call(s32[1,2]{1,0:T(1,128)} %wind_in.1, s32[1,2,9]{2,1,0:T(2,128)} %bitcast.1, f32[1,128,512]{2,1,0:T(8,128)} %layers.1, bf16[9,2,128,512]{3,2,1,0:T(8,128)(2,1)} %weights.1, s32[128,512]{1,0:T(8,128)} %sub_index.1), custom_call_target="tpu_custom_call" | custom-call | tf_op jit(solution)/shard_map/pallas_call | solution.py:320
  16.2 0.7 %copy.7 = f32[2,9,16,64]{3,2,1,0:T(8,128)} copy(f32[2,9,16,64]{3,2,1,0:T(8,128)S(1)} %shard_map.55) | data formatting | bytes 147456

commit v7 on v6

--- a/solution.py
+++ b/solution.py
@@ -17,7 +17,7 @@
 
 def kernel(
     sizes, wind_in, offsets_in, layers, weights, sub_index, out, wind, offsets, raw, wraw, sub, field, mixed,
-    shifted, live, wlive, totals, parts, local_sem, zs_sem, zr_sem, xs_sem, xr_sem, cs_sem, cr_sem, ss_sem, sr_sem, ready,
+    shifted, live, wlive, totals, parts, local_sem, zs_sem, zr_sem, xs_sem, xr_sem, cs_sem, cr_sem, ss_sem, sr_sem, ready, near,
 ):
     n_layer, n_tx, n_ty = sizes
     rows, cols = sub_index.shape
@@ -32,18 +32,43 @@
     down = {"tx": lax.rem(tx + 1, n_tx)}
     left = {"ty": lax.rem(ty + n_ty - 1, n_ty)}
     right = {"ty": lax.rem(ty + 1, n_ty)}
-    peers = [{"layer": layer ^ k} for k in range(n_layer - 1, 0, -1)]
+    peers = [{"layer": layer ^ k} for k in [*range(2, n_layer), 1]]
     row_peers = [(down, 1)] if n_tx == 2 else [(down, 1), (up, 2)]
     col_peers = [(right, cols, 0), (left, PAD, PAD + cols)]
     stages = [1, 0] + list(range(2, tiles))
     cut = [PAD, 2 * PAD] + [PAD + (c + 1) * LANES + PAD for c in range(1, tiles - 1)] + [PAD + cols]
     chunks = list(zip(cut[:-1], cut[1:]))
 
+    barrier = pltpu.get_barrier_semaphore()
+    def signal(semaphore, devices):
+        for device in devices:
+            pl.semaphore_signal(semaphore, inc=1, device_id=device, device_id_type=MESH)
+
+    at_right = [right] + [{**a, **right} for a, _ in row_peers]
+    at_left = [left] + [{**a, **left} for a, _ in row_peers]
+    same = [device for device, _ in row_peers]
+    ahead_right = ty != 0
+    ahead_left = ty == 1
+    signal(barrier, same)
     order = [0, tiles - 1] + list(range(1, tiles - 1))
     own = {}
     for c in order:
         own[c] = pltpu.make_async_copy(layers.at[0, :, pl.ds(c * LANES, LANES)], raw.at[c], local_sem.at[c])
         own[c].start()
+    for device in peers:
+
+        @pl.when(device["layer"] > layer)
+        def _(device=device):
+            signal(barrier, [device])
+
+    @pl.when(ty != 1)
+    def _():
+        signal(barrier, at_left)
+
+    @pl.when(ty == 0)
+    def _():
+        signal(barrier, at_right)
+
     local = [
         pltpu.make_async_copy(wind_in, wind, local_sem.at[tiles]),
         pltpu.make_async_copy(offsets_in, offsets, local_sem.at[tiles + 1]),
@@ -53,26 +78,6 @@
     for copy in local:
         copy.start()
 
-    barrier = pltpu.get_barrier_semaphore()
-    def signal(semaphore, devices):
-        for device in devices:
-            pl.semaphore_signal(semaphore, inc=1, device_id=device, device_id_type=MESH)
-
-    at_right = [right] + [{**a, **right} for a, _ in row_peers]
-    at_left = [left] + [{**a, **left} for a, _ in row_peers]
-    same = [device for device, _ in row_peers] + peers
-    ahead_right = ty != 0
-    ahead_left = ty == 1
-    signal(barrier, same)
-
-    @pl.when(ty != 1)
-    def _():
-        signal(barrier, at_left)
-
-    @pl.when(ty == 0)
-    def _():
-        signal(barrier, at_right)
-
     def turn_tile(c):
         own[c].wait()
         field[0, pl.ds(PAD + c * LANES, LANES), :] = raw[c].T
@@ -80,7 +85,7 @@
     turn_tile(0)
     pl.semaphore_wait(
         barrier,
-        len(same) + len(at_right) * ahead_right.astype(jnp.int32) + len(at_left) * ahead_left.astype(jnp.int32),
+        len(same) + layer + len(at_right) * ahead_right.astype(jnp.int32) + len(at_left) * ahead_left.astype(jnp.int32),
     )
 
     def plan(src, dst, send_sem, recv_sem, device):
@@ -121,6 +126,12 @@
     row_copies = [send_rows(0)]
     turn_tile(tiles - 1)
 
+    for device in peers:
+
+        @pl.when(device["layer"] < layer)
+        def _(device=device):
+            signal(near, [device])
+
     @pl.when(ahead_right)
     def _():
         signal(ready, [right])
@@ -171,12 +182,11 @@
         start_all(col_copies[0])
 
     col_copies[1][0].start()
-    for c in stages[2:-1]:
-        prepare_all(c)
     for copy in row_copies[0]:
         copy.wait_recv()
     start_all(col_copies[1][1:])
-    prepare_all(stages[-1])
+    for c in stages[2:]:
+        prepare_all(c)
 
     def mix(start, end):
         for at in range(start, end, SUB):
@@ -222,9 +232,9 @@
                 sums[s] = term if r == 0 else sums[s] + term
         for s in range(2):
             item = 2 * d + s
-            place = 2 * SUB * stages.index(c) + (item & SUB) + ((item + c) & (SUB - 1))
+            place = 2 * SUB * stages.index(c) + (item & SUB) + ((item + c) & (SUB - 1)) + (SUB if c == stages[-1] else 0)
             if d == DIRS - 1:
-                place = 2 * SUB * tiles + s * tiles + c
+                place = 2 * SUB * (tiles - 1) + s * tiles + c
             back = pltpu.roll(sums[s], (-turn) & (LANES - 1), 1)
             high = back.astype(jnp.bfloat16)
             low = (back - high.astype(jnp.float32)).astype(jnp.bfloat16)
@@ -240,6 +250,10 @@
     for t in range(len(row_peers) + 1):
         mixed[t, pl.ds(0, SUB), :] = jnp.zeros((SUB, LANES), jnp.float32)
     lines = [(2 * LANES * i, 2 * LANES) for i in range(tiles - 1)] + [(2 * LANES * (tiles - 1), 3 * LANES)]
+    @pl.when(layer < n_layer - 1)
+    def _():
+        pl.semaphore_wait(near, n_layer - 1 - layer)
+
     sum_copies = []
     for i, c in enumerate(stages):
         if c:
@@ -259,12 +273,15 @@
                 copy.wait_recv()
             mix(PAD + cols, 2 * PAD + cols)
         sum_copies.append([])
-        edges = [0, DIRS - 1] if i < tiles - 1 else [0, SUB // 2, DIRS - 1]
-        for n, (low, high) in enumerate(zip(edges[:-1], edges[1:])):
-            last = i == tiles - 1 and high == DIRS - 1
-            for d in range(low, high + 1 if last or i < tiles - 1 else high):
+        every = list(range(DIRS - 1))
+        halves = [every[: SUB // 2] + [DIRS - 1], every[SUB // 2 :]] if i == tiles - 1 else [every + [DIRS - 1]]
+        begin = 2 * LANES * i
+        for n, half in enumerate(halves):
+            for d in half:
                 slopes(c, d)
-            line = pl.ds(2 * LANES * i + 2 * low // SUB * LANES, ((2 * high - 2 * low) // SUB + last) * LANES)
+            size = LANES if n else 2 * LANES
+            line = pl.ds(begin, size)
+            begin += size
             parts[layer, :, line] = lax.dot_general(
                 pick, totals[line, :], (((1,), (1,)), ((), ())), preferred_element_type=jnp.float32
             )
@@ -272,6 +289,8 @@
             sum_copies[i] += [
                 send(block, block, ss_sem.at[k, i + n], sr_sem.at[k, i + n], peers[k]) for k in range(n_layer - 1)
             ]
+    for copy in col_copies[0] + col_copies[1] + sum(row_copies, []) + sum(sum_copies[:-1], []):
+        copy.wait_send()
     whole = {}
     for i, c in enumerate(stages):
         for copy in sum_copies[i]:
@@ -289,17 +308,18 @@
             block = None
             for c in range(tiles):
                 slot = (first + c) & (SUB - 1)
-                piece = whole[c][:, item // SUB * LANES : (item // SUB + 1) * LANES]
+                tile = item // SUB + (c == stages[-1])
+                piece = whole[c][:, tile * LANES : (tile + 1) * LANES]
                 inside = (lane_g >= slot * part) & (lane_g < (slot + 1) * part)
                 block = piece if block is None else jnp.where(inside, piece, block)
             if first:
                 block = pltpu.roll(block, LANES - first * part, 1)
             out[s, d] = block[:, :wide]
-    block = whole[tiles - 1][:, 2 * LANES :]
+    block = whole[tiles - 1][:, :LANES]
     out[0, DIRS - 1] = block[:, :wide]
     out[1, DIRS - 1] = block[:, wide:]
 
-    for copy in col_copies[0] + col_copies[1] + sum(row_copies, []) + sum(sum_copies, []):
+    for copy in sum_copies[-1]:
         copy.wait_send()
 
 
@@ -345,6 +365,7 @@
             dma((sizes[0] - 1, tiles + 1)),
             dma((sizes[0] - 1, tiles + 1)),
             pltpu.SemaphoreType.REGULAR,
+            pltpu.SemaphoreType.REGULAR,
         ],
         compiler_params=pltpu.CompilerParams(
             collective_id=0, has_side_effects=True, vmem_limit_bytes=32 * 1024 * 1024

time: 17 us -> 16.8 us (0.988)
  Pallas kernels: 16.2 us -> 15.9 us
    pallas_call x1, Pallas kernels: 16.2 us -> 15.9 us  [on_device(): pl.pallas_call(functools.partial(kernel, sizes), out_shape=pltpu.VMEM((2,...]
where the time goes in v7:
time: 16.8 us; the launch traced here: 16.6 us
  Pallas kernels  15.9 us (95%)
  local copies, waits for them, and re-layouts  0.66 us (4%)
    pallas_call x1, Pallas kernels, on_device(): pl.pallas_call(functools.partial(kernel, sizes), out_shape=pltpu.VMEM((2,...  15.9 us
    unnamed x1, local copies, waits for them, and re-layouts  0.66 us

profile of v7, /device:TPU:0, one launch (start us, length us, event | category | flops | bytes accessed | tf_op | source)
XLA Modules:
  0.0 16.6 jit_solution(14473470885184603888)
XLA Ops:
  0.0 15.9 %shard_map.55 = f32[2,9,16,64]{3,2,1,0:T(8,128)S(1)} custom-call(s32[1,2]{1,0:T(1,128)} %wind_in.1, s32[1,2,9]{2,1,0:T(2,128)} %bitcast.1, f32[1,128,512]{2,1,0:T(8,128)} %layers.1, bf16[9,2,128,512]{3,2,1,0:T(8,128)(2,1)} %weights.1, s32[128,512]{1,0:T(8,128)} %sub_index.1), custom_call_target="tpu_custom_call" | custom-call | tf_op jit(solution)/shard_map/pallas_call | solution.py:340
  16.0 0.7 %copy.7 = f32[2,9,16,64]{3,2,1,0:T(8,128)} copy(f32[2,9,16,64]{3,2,1,0:T(8,128)S(1)} %shard_map.55) | data formatting | bytes 147456

commit v8 on v7

--- a/solution.py
+++ b/solution.py
@@ -256,6 +256,10 @@
 
     sum_copies = []
     for i, c in enumerate(stages):
+        if c == tiles - 1:
+            for copy in col_copies[1]:
+                copy.wait_recv()
+            mix(PAD + cols, 2 * PAD + cols)
         if c:
             for copy in row_copies[c]:
                 copy.wait_recv()
@@ -269,9 +273,7 @@
         else:
             mix(*chunks[c])
         if c == tiles - 1:
-            for copy in col_copies[1]:
-                copy.wait_recv()
-            mix(PAD + cols, 2 * PAD + cols)
+            mix(PAD + cols, PAD + cols + SUB)
         sum_copies.append([])
         every = list(range(DIRS - 1))
         halves = [every[: SUB // 2] + [DIRS - 1], every[SUB // 2 :]] if i == tiles - 1 else [every + [DIRS - 1]]

time: 16.8 us -> 16.8 us (level)
  no operation moved by 1% of the time
where the time goes in v8:
time: 16.8 us; the launch traced here: 16.6 us
  Pallas kernels  15.9 us (95%)
  local copies, waits for them, and re-layouts  0.66 us (4%)
    pallas_call x1, Pallas kernels, on_device(): pl.pallas_call(functools.partial(kernel, sizes), out_shape=pltpu.VMEM((2,...  15.9 us
    unnamed x1, local copies, waits for them, and re-layouts  0.66 us

profile of v8, /device:TPU:0, one launch (start us, length us, event | category | flops | bytes accessed | tf_op | source)
XLA Modules:
  0.0 16.6 jit_solution(4934074089326219504)
XLA Ops:
  0.0 15.9 %shard_map.55 = f32[2,9,16,64]{3,2,1,0:T(8,128)S(1)} custom-call(s32[1,2]{1,0:T(1,128)} %wind_in.1, s32[1,2,9]{2,1,0:T(2,128)} %bitcast.1, f32[1,128,512]{2,1,0:T(8,128)} %layers.1, bf16[9,2,128,512]{3,2,1,0:T(8,128)(2,1)} %weights.1, s32[128,512]{1,0:T(8,128)} %sub_index.1), custom_call_target="tpu_custom_call" | custom-call | tf_op jit(solution)/shard_map/pallas_call | solution.py:342
  15.9 0.7 %copy.7 = f32[2,9,16,64]{3,2,1,0:T(8,128)} copy(f32[2,9,16,64]{3,2,1,0:T(8,128)S(1)} %shard_map.55) | data formatting | bytes 147456
